TPU v7x, 256 devices: a whole 4x4x8 slice. The times are simulated.
256 devices in a mesh: prow: 16 (over x, y), pcol: 16 (over z, core).
Axes of the slice: x: 4, y: 4, z: 8, core: 2. Of those that a mesh axis runs over, the one named last changes fastest.
Arguments:
- known_inverse: bfloat16 [32768, 16, 16, 128], P('prow', None, 'pcol'), may hold values from -6 to 6
- pattern: int32 [256, 16, 16, 1], P('prow', None, 'pcol'), may hold values 0 or 1
- panel_one: bfloat16 [32768, 512], P(('prow', 'pcol')), may hold values from -0.03125 to 0.03125
- panel_two: bfloat16 [32768, 512], P(('prow', 'pcol')), may hold values from -0.03125 to 0.03125
- panel_top: bfloat16 [512, 512], replicated, may hold values from -0.25 to 0.25
- structure: int32 [32768], P(('prow', 'pcol')), may hold values from 0 to 1, as said below
- diag_one: bfloat16 [512, 512], replicated, may hold values from -6 to 6
- diag_two: bfloat16 [512, 512], replicated, may hold values from -6 to 6
Outputs:
- inverse_one: bfloat16 [32768, 512], P(('prow', 'pcol'))
- corner_one: bfloat16 [512, 512], replicated
- inverse_top: bfloat16 [512, 512], replicated
- inverse_two: bfloat16 [32768, 512], P(('prow', 'pcol'))
- corner_two: bfloat16 [512, 512], replicated
Inputs may be any that keep to these rules, and one draw needn't show every extreme that they name: `structure`: in every aligned pair of rows (2 k and 2 k + 1) at least one entry is 1.
All inputs are finite; a program needn't handle non-finite values. No bound on the sum of `pattern` on one device may be relied on, other than what follows from the above.
Results may differ from a plain program's by a relative error of at most 0.0058.
Values may be sent and summed in bfloat16 or wider, within the bound.
A program may use at most 128 MiB of HBM per device.

v0:
```python
import jax
import jax.numpy as jnp
from jax import lax
from jax.sharding import PartitionSpec as P

BLK = 128


def on_device(
    known_inverse, pattern, panel_one, panel_two, panel_top, structure, diag_one, diag_two
):
    row_count = known_inverse.shape[0]
    col_groups = known_inverse.shape[1]
    piece_rows = known_inverse.shape[3]
    block_rows = row_count // BLK
    piece_blocks = piece_rows // BLK
    shaped = known_inverse.reshape(block_rows, BLK, col_groups, piece_blocks, BLK)
    flag_table = pattern.reshape(block_rows, 1, col_groups, piece_blocks, 1)
    masked = jnp.where(flag_table > 0, shaped, jnp.zeros_like(shaped)).reshape(
        row_count, col_groups * piece_rows
    )
    row_flags = structure.reshape(piece_rows, 1) > 0
    masked_two = jnp.where(row_flags, panel_two, jnp.zeros_like(panel_two))

    def accumulate(pieces):
        return jnp.dot(masked, pieces, preferred_element_type=jnp.float32)

    partial_one = accumulate(lax.all_gather(panel_one, "prow", axis=0, tiled=True))
    reduced_one = lax.psum_scatter(partial_one, "pcol", scatter_dimension=0, tiled=True)
    partial_two = accumulate(lax.all_gather(masked_two, "prow", axis=0, tiled=True))
    reduced_two = lax.psum_scatter(partial_two, "pcol", scatter_dimension=0, tiled=True)
    inverse_one = (-reduced_one).astype(jnp.bfloat16)
    own_term = jnp.dot(panel_one.T, inverse_one, preferred_element_type=jnp.float32)
    cross_local = jnp.dot(inverse_one.T, masked_two, preferred_element_type=jnp.float32)
    lower_two = -(reduced_two + jnp.dot(inverse_one, panel_top, preferred_element_type=jnp.float32))
    inverse_two = jnp.where(row_flags, lower_two, jnp.zeros_like(lower_two)).astype(jnp.bfloat16)
    tail_local = jnp.dot(masked_two.T, inverse_two, preferred_element_type=jnp.float32)
    top_weights = panel_top.astype(jnp.float32)
    own_sum, cross_sum = lax.psum((own_term, cross_local), ("prow", "pcol"))
    corner_full = diag_one.astype(jnp.float32) - own_sum
    top_value = jnp.dot(corner_full, top_weights, precision=lax.Precision.HIGHEST) + cross_sum
    inverse_top = (-top_value).astype(jnp.bfloat16)
    tail_sum = lax.psum(tail_local, ("prow", "pcol"))
    corner_two = (
        diag_two.astype(jnp.float32)
        - jnp.dot(panel_top.T, inverse_top, preferred_element_type=jnp.float32)
        - tail_sum
    )
    return (
        inverse_one,
        corner_full.astype(jnp.bfloat16),
        inverse_top,
        inverse_two,
        corner_two.astype(jnp.bfloat16),
    )


def solution(mesh):
    in_specs = (
        P("prow", None, "pcol", None),
        P("prow", None, "pcol", None),
        P(("prow", "pcol"), None),
        P(("prow", "pcol"), None),
        P(),
        P(("prow", "pcol")),
        P(),
        P(),
    )
    out_specs = (P(("prow", "pcol"), None), P(), P(), P(("prow", "pcol"), None), P())
    return jax.shard_map(
        on_device, mesh=mesh, in_specs=in_specs, out_specs=out_specs, check_vma=False
    )
```

profile of v0, /device:TPU:8, one launch (start us, length us, event | category | flops | bytes accessed | tf_op | source)
XLA Modules:
  0.0 526.8 jit_solution(959092906501539637)
XLA Ops:
  7.2 0.0 copy-start
  7.2 0.0 all-gather.3.cloned.1.call-start
  7.2 0.7 all-gather.3.cloned.1.call-update
  7.9 0.0 all-gather.5.cloned.1.call-start
  8.0 0.7 broadcast_compare_fusion.1
  8.6 1.6 broadcast_select_fusion
  10.3 0.0 all-gather.5.cloned.1.call-update
  10.3 0.0 reduce-scatter.3.cloned.1.call-start
  10.3 0.7 broadcast_compare_fusion
  11.1 51.9 %all-gather.3.cloned.1.call-done = bf16[2048,512]{1,0:T(8,128)(2,1)} async-done(((bf16[128,512]{1,0:T(8,128)(2,1)}), bf16[2048,512]{1,0:T(8,128)(2,1)}) %all-gather.3.cloned.1.call-update) | async-done | bytes 2097168 | tf_op jit(solution)/shard_map/all_gather | solution.py:28
  63.0 1.1 broadcast_in_dim.33
  64.1 0.0 copy-start.1
  64.1 2.0 copy-done.1
  66.1 0.0 copy-done.10
  66.1 10.0 %fusion.1 = f32[2048,512]{1,0:T(8,128)} fusion(bf16[2048,512]{1,0:T(8,128)(2,1)S(1)} %copy-done.10, pred[256,8,16,128]{3,2,1,0:T(8,128)(4,1)S(1)} %bitcast.40, bf16[256,8,16,128]{3,2,1,0:T(8,128)(2,1)} %bitcast.43), kind=kOutput, calls=%fused_computation.2 | convolution fusion | flops 4299161600 | bytes 18874368 | tf_op jit(solution)/shard_map/dot_general | solution.py:26
  76.1 0.0 reduce-scatter.3.cloned.1.call-update
  76.1 0.0 reduce-scatter.5.cloned.1.call-start
  76.2 39.2 %all-gather.5.cloned.1.call-done = bf16[2048,512]{1,0:T(8,128)(2,1)} async-done(((bf16[128,512]{1,0:T(8,128)(2,1)}), bf16[2048,512]{1,0:T(8,128)(2,1)}) %all-gather.5.cloned.1.call-update) | async-done | bytes 2097168 | tf_op jit(solution)/shard_map/all_gather | solution.py:30
  115.4 11.7 %fusion = f32[2048,512]{1,0:T(8,128)} fusion(bf16[2048,512]{1,0:T(8,128)(2,1)} %all-gather.5.cloned.1.call-done, pred[256,8,16,128]{3,2,1,0:T(8,128)(4,1)} %bitcast.41, bf16[256,8,16,128]{3,2,1,0:T(8,128)(2,1)} %bitcast.44), kind=kOutput, calls=%fused_computation.1 | convolution fusion | flops 4299161600 | bytes 18874368 | tf_op jit(solution)/shard_map/dot_general | solution.py:26
  127.1 0.0 reduce-scatter.5.cloned.1.call-update
  127.1 0.0 copy-start.7
  127.1 0.2 all-reduce.3.cloned.1.call-start
  127.3 53.2 %reduce-scatter.3.cloned.1.call-done = f32[128,512]{1,0:T(8,128)} async-done(((f32[2048,512]{1,0:T(8,128)}), f32[128,512]{1,0:T(8,128)}) %reduce-scatter.3.cloned.1.call-update) | async-done | bytes 262160 | tf_op jit(solution)/shard_map/reduce_scatter | solution.py:29
  180.6 1.0 negate_convert_fusion
  181.5 0.0 copy-done.2
  181.5 0.0 copy-start.4
  181.6 1.3 fusion.13
  182.9 0.0 copy-done.6
  182.9 1.3 convolution_bitcast_fusion.1
  184.2 59.9 %reduce-scatter.5.cloned.1.call-done = f32[128,512]{1,0:T(8,128)} async-done(((f32[2048,512]{1,0:T(8,128)}), f32[128,512]{1,0:T(8,128)}) %reduce-scatter.5.cloned.1.call-update) | async-done | bytes 262160 | tf_op jit(solution)/shard_map/reduce_scatter | solution.py:31
  244.1 0.0 copy-done
  244.1 1.2 fusion.9
  245.3 0.0 copy-start.9
  245.3 1.3 fusion.14
  246.7 0.0 all-reduce.3.cloned.1.call-update
  246.7 0.0 copy-done.7
  246.7 0.2 copy.13
  246.9 0.0 copy-done.4
  246.9 0.0 copy-done.8
  246.9 0.2 copy.14
  247.2 266.5 %all-reduce.3.cloned.1.call-done = (f32[512,512]{0,1:T(8,128)}, f32[512,512]{1,0:T(8,128)}, f32[512,512]{0,1:T(8,128)}) async-done(((f32[512,512]{0,1:T(8,128)}, f32[512,512]{1,0:T(8,128)}, f32[512,512]{0,1:T(8,128)}), (f32[512,512]{0,1:T(8,128)}, f32[512,512]{1,0:T(8,128)}, f32[512,512]{0,1:T(8,128)})) %all-reduce.3.cloned.1.call-update) | async-done | bytes 3145744 | tf_op jit(solution)/shard_map/psum | solution.py:39
  513.7 1.5 fusion.10
  515.1 2.6 fusion.5
  517.7 0.0 copy-start.3
  517.7 0.5 fusion.6
  518.2 1.0 copy.17
  519.2 1.0 copy.16
  520.2 0.0 copy-done.3
  (8 shorter events, 0.0 us)
Async XLA Ops:
  7.2 237.0 %copy-start = (bf16[512,512]{1,0:T(8,128)(2,1)S(1)}, bf16[512,512]{1,0:T(8,128)(2,1)}, u32[]{:S(2)}) copy-start(bf16[512,512]{1,0:T(8,128)(2,1)} %param.12) | copy-start | bytes 1572868
  7.2 55.8 %all-gather.3.cloned.1.call-start = ((), (), s32[]{:S(2)}) async-start(), calls=%async_computation.2 | async-start | bytes 2228224 | tf_op jit(solution)/shard_map/all_gather | solution.py:28
  7.9 107.5 %all-gather.5.cloned.1.call-start = ((), (), s32[]{:S(2)}) async-start(), calls=%async_computation.4 | async-start | bytes 2228224 | tf_op jit(solution)/shard_map/all_gather | solution.py:30
  10.3 170.3 %reduce-scatter.3.cloned.1.call-start = ((), (), s32[]{:S(2)}) async-start(), calls=%async_computation.3 | async-start | bytes 4456448 | tf_op jit(solution)/shard_map/reduce_scatter | solution.py:29
  63.0 3.1 copy-start.10
  64.1 2.0 copy-start.1
  76.1 168.0 %reduce-scatter.5.cloned.1.call-start = ((), (), s32[]{:S(2)}) async-start(), calls=%async_computation.5 | async-start | bytes 4456448 | tf_op jit(solution)/shard_map/reduce_scatter | solution.py:31
  127.1 54.5 %copy-start.2 = (bf16[128,512]{1,0:T(8,128)(2,1)S(1)}, bf16[128,512]{1,0:T(8,128)(2,1)}, u32[]{:S(2)}) copy-start(bf16[128,512]{1,0:T(8,128)(2,1)} %broadcast_select_fusion) | copy-start | bytes 393220
  127.1 55.8 %copy-start.6 = (bf16[128,512]{1,0:T(8,128)(2,1)S(1)}, bf16[128,512]{1,0:T(8,128)(2,1)}, u32[]{:S(2)}) copy-start(bf16[128,512]{1,0:T(8,128)(2,1)} %param.10) | copy-start | bytes 393220
  127.1 119.6 %copy-start.7 = (bf16[512,512]{1,0:T(8,128)(2,1)S(1)}, bf16[512,512]{1,0:T(8,128)(2,1)}, u32[]{:S(2)}) copy-start(bf16[512,512]{1,0:T(8,128)(2,1)} %param.14) | copy-start | bytes 1572868
  127.1 386.5 %all-reduce.3.cloned.1.call-start = ((), (), s32[]{:S(2)}) async-start(), calls=%async_computation.6 | async-start | bytes 6291456 | tf_op jit(solution)/shard_map/psum | solution.py:39
  181.5 65.4 %copy-start.4 = (bf16[128,512]{1,0:T(8,128)(2,1)}, bf16[128,512]{1,0:T(8,128)(2,1)S(1)}, u32[]{:S(2)}) copy-start(bf16[128,512]{1,0:T(8,128)(2,1)S(1)} %negate_convert_fusion) | copy-start | bytes 393220
  182.9 64.0 %copy-start.8 = (bf16[512,512]{1,0:T(8,128)(2,1)S(1)}, bf16[512,512]{1,0:T(8,128)(2,1)}, u32[]{:S(2)}) copy-start(bf16[512,512]{1,0:T(8,128)(2,1)} %param.15) | copy-start | bytes 1572868
  245.3 269.8 %copy-start.9 = (bf16[128,512]{1,0:T(8,128)(2,1)}, bf16[128,512]{1,0:T(8,128)(2,1)S(1)}, u32[]{:S(2)}) copy-start(bf16[128,512]{1,0:T(8,128)(2,1)S(1)} %fusion.9) | copy-start | bytes 393220
  513.7 4.1 copy-start.5
  517.7 2.5 copy-start.3
Sparse Core Ops, SparseCore 0:
  10.4 52.4 all-gather.2
  66.0 49.3 all-gather.4
  117.9 62.5 reduce-scatter.2
  183.0 61.1 reduce-scatter.4
  249.7 263.8 all-reduce.2
where the time goes:
time: 527 us
  waiting for transfers between devices  472 us (90%)
  matrix products  29.8 us (6%)
  between operations  13.9 us (3%)
  local copies, waits for them, and re-layouts  5.61 us (1%)
  other arithmetic  5.46 us (1%)
    psum x1, waiting for transfers between devices, on_device(): own_sum, cross_sum = lax.psum((own_term, cross_local), ('prow', 'pcol'))  266 us
    reduce_scatter x1, waiting for transfers between devices, on_device(): lax.psum_scatter(partial_two, 'pcol', scatter_dimension=0, tiled=True)  59.9 us
    reduce_scatter x1, waiting for transfers between devices, on_device(): lax.psum_scatter(partial_one, 'pcol', scatter_dimension=0, tiled=True)  53.2 us
    all_gather x1, waiting for transfers between devices, on_device(): lax.all_gather(panel_one, 'prow', axis=0, tiled=True)  51.9 us
    all_gather x1, waiting for transfers between devices, on_device(): lax.all_gather(masked_two, 'prow', axis=0, tiled=True)  39.2 us
    dot_general x2, matrix products, accumulate(): return jnp.dot(masked, pieces, preferred_element_type=jnp.float32)  21.7 us
  transfers between devices with their start and end apart: 5, of which 5 were waited for; matrix products, arithmetic and copies ran while one was open for 6% of the time, Pallas kernels for 0%

commit v1 on v0

--- a/solution.py
+++ b/solution.py
@@ -25,7 +25,11 @@
     def accumulate(pieces):
         return jnp.dot(masked, pieces, preferred_element_type=jnp.float32)
 
-    partial_one = accumulate(lax.all_gather(panel_one, "prow", axis=0, tiled=True))
+    partial_one = accumulate(
+        jnp.concatenate(
+            lax.all_to_all(jnp.stack([panel_one] * lax.axis_size("prow")), "prow", 0, 0), axis=0
+        )
+    )
     reduced_one = lax.psum_scatter(partial_one, "pcol", scatter_dimension=0, tiled=True)
     partial_two = accumulate(lax.all_gather(masked_two, "prow", axis=0, tiled=True))
     reduced_two = lax.psum_scatter(partial_two, "pcol", scatter_dimension=0, tiled=True)

time: 527 us -> 469 us (0.89)
  waiting for transfers between devices: 472 us -> 399 us
  starting transfers between devices: 0.38 us -> 7.73 us
  other arithmetic: 5.46 us -> 12 us
    all_gather x1 -> x0, waiting for transfers between devices: 51.9 us -> none  [on_device(): lax.all_gather(panel_one, 'prow', axis=0, tiled=True)]
    all_to_all x0 -> x1, waiting for transfers between devices: none -> 23.4 us  [on_device(): lax.all_to_all(jnp.stack([panel_one] * lax.axis_size('prow')), 'prow', 0, 0)]
    all_gather x1, waiting for transfers between devices: 39.2 us -> 16.7 us  [on_device(): lax.all_gather(masked_two, 'prow', axis=0, tiled=True)]
    reduce_scatter x1, waiting for transfers between devices: 53.2 us -> 34.6 us  [on_device(): lax.psum_scatter(partial_one, 'pcol', scatter_dimension=0, tiled=True)]
    all_to_all x0 -> x1, starting transfers between devices: none -> 7.39 us  [on_device(): lax.all_to_all(jnp.stack([panel_one] * lax.axis_size('prow')), 'prow', 0, 0)]
    select_n x0 -> x1, other arithmetic: none -> 7.23 us  [on_device(): jnp.where(flag_table > 0, shaped, jnp.zeros_like(shaped))]
  transfers between devices with their start and end apart: 5 -> 5, of which waited for: 5 -> 5; matrix products, arithmetic and copies ran while one was open for 6% -> 7% of each run, Pallas kernels for 0% -> 0%
where the time goes in v1:
time: 469 us
  waiting for transfers between devices  399 us (85%)
  matrix products  27.8 us (6%)
  between operations  15.7 us (3%)
  other arithmetic  12 us (3%)
  starting transfers between devices  7.73 us (2%)
  local copies, waits for them, and re-layouts  6.62 us (1%)
    psum x1, waiting for transfers between devices, on_device(): own_sum, cross_sum = lax.psum((own_term, cross_local), ('prow', 'pcol'))  264 us
    reduce_scatter x1, waiting for transfers between devices, on_device(): lax.psum_scatter(partial_two, 'pcol', scatter_dimension=0, tiled=True)  60 us
    reduce_scatter x1, waiting for transfers between devices, on_device(): lax.psum_scatter(partial_one, 'pcol', scatter_dimension=0, tiled=True)  34.6 us
    all_to_all x1, waiting for transfers between devices, on_device(): lax.all_to_all(jnp.stack([panel_one] * lax.axis_size('prow')), 'prow', 0, 0)  23.4 us
    dot_general x2, matrix products, accumulate(): return jnp.dot(masked, pieces, preferred_element_type=jnp.float32)  19.6 us
    all_gather x1, waiting for transfers between devices, on_device(): lax.all_gather(masked_two, 'prow', axis=0, tiled=True)  16.7 us
  transfers between devices with their start and end apart: 5, of which 5 were waited for; matrix products, arithmetic and copies ran while one was open for 7% of the time, Pallas kernels for 0%

profile of v1, /device:TPU:8, one launch (start us, length us, event | category | flops | bytes accessed | tf_op | source)
XLA Modules:
  0.0 468.7 jit_solution(905020512684259783)
XLA Ops:
  8.0 0.0 copy-start
  8.0 0.0 copy-start.9
  8.0 0.0 all-gather.2.cloned.1.call-start
  8.1 0.7 broadcast_compare_fusion.1
  8.8 1.6 broadcast_select_fusion.1
  10.4 0.0 all-gather.2.cloned.1.call-update
  10.4 2.5 stack.2
  12.9 7.4 %all-to-all-start = ((bf16[16,128,512]{2,1,0:T(8,128)(2,1)}), bf16[16,128,512]{2,1,0:T(8,128)(2,1)S(1)}, u32[]{:S(2)}, u32[]{:S(2)}) async-start(bf16[16,128,512]{2,1,0:T(8,128)(2,1)} %stack.2), calls=%async_computation | async-start | bytes 4194304 | tf_op jit(solution)/shard_map/all_to_all | solution.py:30
  20.3 0.0 reduce-scatter.3.cloned.1.call-start
  20.4 0.0 copy-done.9
  20.4 7.2 %broadcast_select_fusion = bf16[16,128,16,1,128]{4,2,1,0,3:T(8,128)(2,1)} fusion(bf16[16,128,16,1,128]{4,2,1,0,3:T(8,128)(2,1)} %bitcast.48, pred[16,16]{1,0:T(8,128)(4,1)S(1)} %bitcast.53), kind=kLoop, calls=%fused_computation.7 | loop fusion | flops 4194304 | bytes 16777472 | tf_op jit(solution)/shard_map/jit(_where)/select_n | solution.py:19
  27.7 23.4 %all-to-all-done = bf16[16,128,512]{2,1,0:T(8,128)(2,1)S(1)} async-done(((bf16[16,128,512]{2,1,0:T(8,128)(2,1)}), bf16[16,128,512]{2,1,0:T(8,128)(2,1)S(1)}, u32[]{:S(2)}, u32[]{:S(2)}) %all-to-all-start) | async-done | bytes 2097184 | tf_op jit(solution)/shard_map/all_to_all | solution.py:30
  51.1 9.6 %fusion.3 = f32[2048,512]{1,0:T(8,128)} fusion(bf16[2048,512]{1,0:T(8,128)(2,1)S(1)} %bitcast.52, bf16[256,8,16,128]{3,2,1,0:T(8,128)(2,1)} %bitcast.50), kind=kOutput, calls=%fused_computation.4 | convolution fusion | flops 4294967296 | bytes 14680064 | tf_op jit(solution)/shard_map/dot_general | solution.py:26
  60.7 0.0 reduce-scatter.3.cloned.1.call-update
  60.7 0.0 reduce-scatter.5.cloned.1.call-start
  60.8 16.7 %all-gather.2.cloned.1.call-done = bf16[2048,512]{1,0:T(8,128)(2,1)} async-done(((bf16[128,512]{1,0:T(8,128)(2,1)}), bf16[2048,512]{1,0:T(8,128)(2,1)}) %all-gather.2.cloned.1.call-update) | async-done | bytes 2097168 | tf_op jit(solution)/shard_map/all_gather | solution.py:34
  77.5 1.1 broadcast_in_dim.35
  78.7 0.5 copy-done.10
  79.1 10.0 %fusion = f32[2048,512]{1,0:T(8,128)} fusion(bf16[2048,512]{1,0:T(8,128)(2,1)S(1)} %copy-done.10, pred[256,8,16,128]{3,2,1,0:T(8,128)(4,1)S(1)} %bitcast.51, bf16[256,8,16,128]{3,2,1,0:T(8,128)(2,1)} %bitcast.49), kind=kOutput, calls=%fused_computation.1 | convolution fusion | flops 4299161600 | bytes 18874368 | tf_op jit(solution)/shard_map/dot_general | solution.py:26
  89.2 0.0 reduce-scatter.5.cloned.1.call-update
  89.2 0.0 copy-start.6
  89.2 0.2 all-reduce.3.cloned.1.call-start
  89.4 34.6 %reduce-scatter.3.cloned.1.call-done = f32[128,512]{1,0:T(8,128)} async-done(((f32[2048,512]{1,0:T(8,128)}), f32[128,512]{1,0:T(8,128)}) %reduce-scatter.3.cloned.1.call-update) | async-done | bytes 262160 | tf_op jit(solution)/shard_map/reduce_scatter | solution.py:33
  124.0 1.0 negate_convert_fusion
  125.0 0.0 copy-done.1
  125.0 0.0 copy-start.3
  125.0 1.3 fusion.17
  126.3 0.0 copy-done.5
  126.3 1.3 convolution_bitcast_fusion.1
  127.6 60.0 %reduce-scatter.5.cloned.1.call-done = f32[128,512]{1,0:T(8,128)} async-done(((f32[2048,512]{1,0:T(8,128)}), f32[128,512]{1,0:T(8,128)}) %reduce-scatter.5.cloned.1.call-update) | async-done | bytes 262160 | tf_op jit(solution)/shard_map/reduce_scatter | solution.py:35
  187.6 0.0 copy-done
  187.6 1.2 fusion.14
  188.8 0.0 copy-start.8
  188.8 1.3 fusion.18
  190.2 0.0 all-reduce.3.cloned.1.call-update
  190.2 0.0 copy-done.6
  190.2 0.2 copy.13
  190.4 0.0 copy-done.3
  190.5 0.0 copy-done.7
  190.5 0.2 copy.14
  190.7 264.0 %all-reduce.3.cloned.1.call-done = (f32[512,512]{0,1:T(8,128)}, f32[512,512]{1,0:T(8,128)}, f32[512,512]{0,1:T(8,128)}) async-done(((f32[512,512]{0,1:T(8,128)}, f32[512,512]{1,0:T(8,128)}, f32[512,512]{0,1:T(8,128)}), (f32[512,512]{0,1:T(8,128)}, f32[512,512]{1,0:T(8,128)}, f32[512,512]{0,1:T(8,128)})) %all-reduce.3.cloned.1.call-update) | async-done | bytes 3145744 | tf_op jit(solution)/shard_map/psum | solution.py:43
  454.7 1.5 fusion.15
  456.2 2.6 fusion.10
  458.7 0.0 copy-start.2
  458.8 0.0 copy-done.4
  458.8 0.5 fusion.11
  459.2 1.0 copy.17
  460.2 1.0 copy.16
  (9 shorter events, 0.0 us)
Async XLA Ops:
  8.0 179.6 %copy-start = (bf16[512,512]{1,0:T(8,128)(2,1)S(1)}, bf16[512,512]{1,0:T(8,128)(2,1)}, u32[]{:S(2)}) copy-start(bf16[512,512]{1,0:T(8,128)(2,1)} %param.12) | copy-start | bytes 1572868
  8.0 12.4 %copy-start.9 = (s32[16,16,1,1]{1,3,2,0:T(1,128)S(1)}, s32[16,16,1,1]{1,3,2,0:T(1,128)}, u32[]{:S(2)}) copy-start(s32[16,16,1,1]{1,3,2,0:T(1,128)} %param.9) | copy-start | bytes 3076
  8.0 69.5 %all-gather.2.cloned.1.call-start = ((), (), s32[]{:S(2)}) async-start(), calls=%async_computation.4 | async-start | bytes 2228224 | tf_op jit(solution)/shard_map/all_gather | solution.py:34
  12.9 38.2 %all-to-all-start = ((bf16[16,128,512]{2,1,0:T(8,128)(2,1)}), bf16[16,128,512]{2,1,0:T(8,128)(2,1)S(1)}, u32[]{:S(2)}, u32[]{:S(2)}) async-start(bf16[16,128,512]{2,1,0:T(8,128)(2,1)} %stack.2), calls=%async_computation | async-start | bytes 4194304 | tf_op jit(solution)/shard_map/all_to_all | solution.py:30
  20.3 103.6 %reduce-scatter.3.cloned.1.call-start = ((), (), s32[]{:S(2)}) async-start(), calls=%async_computation.3 | async-start | bytes 4456448 | tf_op jit(solution)/shard_map/reduce_scatter | solution.py:33
  60.7 126.9 %reduce-scatter.5.cloned.1.call-start = ((), (), s32[]{:S(2)}) async-start(), calls=%async_computation.5 | async-start | bytes 4456448 | tf_op jit(solution)/shard_map/reduce_scatter | solution.py:35
  77.5 1.6 copy-start.10
  89.2 35.8 %copy-start.1 = (bf16[128,512]{1,0:T(8,128)(2,1)S(1)}, bf16[128,512]{1,0:T(8,128)(2,1)}, u32[]{:S(2)}) copy-start(bf16[128,512]{1,0:T(8,128)(2,1)} %broadcast_select_fusion.1) | copy-start | bytes 393220
  89.2 37.2 %copy-start.5 = (bf16[128,512]{1,0:T(8,128)(2,1)S(1)}, bf16[128,512]{1,0:T(8,128)(2,1)}, u32[]{:S(2)}) copy-start(bf16[128,512]{1,0:T(8,128)(2,1)} %param.10) | copy-start | bytes 393220
  89.2 101.0 %copy-start.6 = (bf16[512,512]{1,0:T(8,128)(2,1)S(1)}, bf16[512,512]{1,0:T(8,128)(2,1)}, u32[]{:S(2)}) copy-start(bf16[512,512]{1,0:T(8,128)(2,1)} %param.14) | copy-start | bytes 1572868
  89.2 365.5 %all-reduce.3.cloned.1.call-start = ((), (), s32[]{:S(2)}) async-start(), calls=%async_computation.6 | async-start | bytes 6291456 | tf_op jit(solution)/shard_map/psum | solution.py:43
  125.0 65.5 %copy-start.3 = (bf16[128,512]{1,0:T(8,128)(2,1)}, bf16[128,512]{1,0:T(8,128)(2,1)S(1)}, u32[]{:S(2)}) copy-start(bf16[128,512]{1,0:T(8,128)(2,1)S(1)} %negate_convert_fusion) | copy-start | bytes 393220
  126.3 64.1 %copy-start.7 = (bf16[512,512]{1,0:T(8,128)(2,1)S(1)}, bf16[512,512]{1,0:T(8,128)(2,1)}, u32[]{:S(2)}) copy-start(bf16[512,512]{1,0:T(8,128)(2,1)} %param.15) | copy-start | bytes 1572868
  188.8 267.3 %copy-start.8 = (bf16[128,512]{1,0:T(8,128)(2,1)}, bf16[128,512]{1,0:T(8,128)(2,1)S(1)}, u32[]{:S(2)}) copy-start(bf16[128,512]{1,0:T(8,128)(2,1)S(1)} %fusion.14) | copy-start | bytes 393220
  454.7 4.1 copy-start.4
  458.7 2.5 copy-start.2
Sparse Core Ops, SparseCore 0:
  11.9 65.5 all-gather.1
  190.3 264.2 all-reduce.2
Sparse Core Ops, SparseCore 1:
  60.8 63.1 reduce-scatter.2
  126.4 61.2 reduce-scatter.4
